TPU v7x, 256 devices: a whole 4x4x8 slice. The times are simulated.
256 devices in a mesh: req: 2 (over core), seq: 128 (over y, z, x).
Axes of the slice: x: 4, y: 4, z: 8, core: 2. Of those that a mesh axis runs over, the one named last changes fastest.
Arguments:
- queries: bfloat16 [4, 8192], P('req'), parts along dimension 0, may hold values from -120 to 120
- new_tokens: bfloat16 [4, 2048], P('req'), parts along dimension 0, may hold values from -10.75 to 10.75
- cache_rows: bfloat16 [262144, 2048], P(('req', 'seq')), parts along dimension 0, may hold values from -4 to 4
- cache_length: int32 [2], P('req'), parts along dimension 0, may hold values from 65537 to 131072
- span_rows: bfloat16 [512, 512, 2048], P(('req', 'seq')), parts along dimension 0, may hold values from -6 to 6
- slot_blocks: int32 [512], P('req'), parts along dimension 0, may hold values from -1 to 31, as said below
- decode_owner: int32 [64], P('req'), parts along dimension 0, may hold values from 0 to 127, as said below
Outputs:
- attention: bfloat16 [4, 8192], P('req'), parts along dimension 0
- relaid_blocks: bfloat16 [256, 512, 2048], P(('req', 'seq')), parts along dimension 0
There are 2 independent parts, one for each index of `req`. A program takes and returns all parts, laid end to end along the dimension named above; each array names one. Nothing has to cross between parts.
Inputs may be any that keep to these rules, and one draw needn't show every extreme that they name: `slot_blocks`: each block number 0 .. 31 stands in exactly one slot and -1 in all others; device i holds slots 2 * i .. 2 * i + 1, and some device has all its slots filled. `decode_owner`: the owners of different blocks are different devices.
All inputs are finite; a program needn't handle non-finite values.
Results may differ from a plain program's by a relative error of at most 0.0055.
Values may be sent and summed in bfloat16 or wider, within the bound.
No kernel may reach another device: no remote copies, remote signals or barrier semaphores. Data moves between devices by JAX's collectives and lax.ppermute only.
A program may use at most 128 MiB of HBM per device.

v0:
```python
import jax
import jax.numpy as jnp
from jax import lax
from jax.sharding import PartitionSpec as P

HEAD_DIM = 128


NEGATIVE = -1e30


def attend(queries, key_value, usable):
    step_count = queries.shape[0]
    half_width = key_value.shape[1] // 2
    kv_heads = half_width // HEAD_DIM
    grouped = queries.reshape(step_count, kv_heads, -1, HEAD_DIM)
    key_part = key_value[:, :half_width].reshape(key_value.shape[0], kv_heads, HEAD_DIM)
    value_part = key_value[:, half_width:].reshape(key_value.shape[0], kv_heads, HEAD_DIM)
    scores = jnp.einsum(
        "sghd,rgd->gshr", grouped, key_part, preferred_element_type=jnp.float32
    ) * HEAD_DIM ** (-0.5)
    scores = jnp.where(usable, scores, NEGATIVE)
    highest = jnp.max(scores, axis=3)
    weights = jnp.where(usable, jnp.exp(scores - highest[..., None]), 0.0)
    totals = jnp.sum(weights, axis=3)
    output = jnp.einsum(
        "gshr,rgd->gshd",
        weights.astype(jnp.bfloat16),
        value_part,
        preferred_element_type=jnp.float32,
    )
    return (highest, totals, output)


def combine(earlier, latter):
    highest = jnp.maximum(earlier[0], latter[0])
    first_scale = jnp.exp(earlier[0] - highest)
    second_scale = jnp.exp(latter[0] - highest)
    totals = earlier[1] * first_scale + latter[1] * second_scale
    output = earlier[2] * first_scale[..., None] + latter[2] * second_scale[..., None]
    return (highest, totals, output)


def shards(queries, new_tokens, cache_rows, cache_length, span_rows, slot_blocks, decode_owner):
    devices = lax.axis_size("seq")
    own_index = lax.axis_index("seq")
    slot_count = span_rows.shape[0]
    block_rows = span_rows.shape[1]
    features = span_rows.shape[2]
    piece_rows = block_rows // devices
    step_count = queries.shape[0]
    local_rows = cache_rows.shape[0]
    positions = own_index * local_rows + jnp.arange(local_rows, dtype=jnp.int32)
    partial_value = attend(queries, cache_rows, positions < cache_length[0])
    spread = lax.all_to_all(
        span_rows.reshape(slot_count, devices, piece_rows, features),
        "seq",
        split_axis=1,
        concat_axis=1,
        tiled=True,
    )
    spread_ids = slot_blocks.reshape(devices, slot_count).T.reshape(-1)
    spread_rows = spread.reshape(slot_count * devices, piece_rows, features)
    targets = jnp.arange(devices, dtype=jnp.int32)
    ownership = decode_owner[None, :] == targets[:, None]
    has_block = jnp.any(ownership, axis=1)
    block_of = jnp.argmax(ownership, axis=1)
    row_of = jnp.argmax(spread_ids[None, :] == block_of[:, None], axis=1)
    outgoing = jnp.where(has_block[:, None, None], spread_rows[row_of], jnp.zeros((), jnp.bfloat16))
    arrived = lax.all_to_all(outgoing, "seq", split_axis=0, concat_axis=0, tiled=True)
    relaid = arrived.reshape(block_rows, features)
    holds_block = has_block[own_index]
    partial_value = combine(
        partial_value, attend(queries, relaid, jnp.broadcast_to(holds_block, (block_rows,)))
    )
    highest = lax.pmax(partial_value[0], "seq")
    factor = jnp.exp(partial_value[0] - highest)
    totals, output = lax.psum(
        (partial_value[1] * factor, partial_value[2] * factor[..., None]), "seq"
    )
    merged = (highest, totals, output)
    step_index = jnp.arange(step_count, dtype=jnp.int32)
    causal = step_index[None, :] <= step_index[:, None]
    merged = combine(merged, attend(queries, new_tokens, causal[None, :, None, :]))
    result = merged[2] / merged[1][..., None]
    attention = result.transpose(1, 0, 2, 3).reshape(step_count, -1).astype(jnp.bfloat16)
    return (attention, relaid.reshape(1, block_rows, features))


def solution(mesh):
    placed = (
        P("req", None),
        P("req", None),
        P(("req", "seq"), None),
        P("req"),
        P(("req", "seq"), None, None),
        P("req"),
        P("req"),
    )
    return jax.shard_map(
        shards,
        mesh=mesh,
        in_specs=placed,
        out_specs=(P("req", None), P(("req", "seq"), None, None)),
        check_vma=False,
    )
```

profile of v0, /device:TPU:2, one launch (start us, length us, event | category | flops | bytes accessed | tf_op | source)
XLA Modules:
  0.0 1124.9 jit_solution(2665612077683009008)
XLA Ops:
  7.2 6.5 copy.72
  13.7 6.2 copy.73
  19.9 0.0 copy-start.4
  19.9 0.0 copy-start.6
  19.9 16.0 %all-to-all-start = ((bf16[2,128,4,2048]{3,2,0,1:T(4,128)(2,1)}), bf16[2,128,4,2048]{3,2,0,1:T(4,128)(2,1)}, u32[]{:S(2)}, u32[]{:S(2)}) async-start(bf16[2,128,4,2048]{3,2,0,1:T(4,128)(2,1)} %copy.73), calls=%async_computation | async-start | bytes 8388608 | tf_op jit(solution)/shard_map/all_to_all | solution.py:55
  35.9 0.0 copy-done.4
  35.9 0.1 reshape.82
  36.1 0.1 copy.75
  36.1 0.0 copy-done.6
  36.1 0.6 iota_reduce_fusion.1
  36.7 0.7 iota_reduce_fusion
  37.5 0.1 fusion.25
  37.5 94.5 %all-to-all-done = bf16[2,128,4,2048]{3,2,0,1:T(4,128)(2,1)} async-done(((bf16[2,128,4,2048]{3,2,0,1:T(4,128)(2,1)}), bf16[2,128,4,2048]{3,2,0,1:T(4,128)(2,1)}, u32[]{:S(2)}, u32[]{:S(2)}) %all-to-all-start) | async-done | bytes 4194336 | tf_op jit(solution)/shard_map/all_to_all | solution.py:55
  132.1 6.7 copy.74
  138.8 4.5 gather_fusion
  143.3 2.3 broadcast_select_fusion
  145.7 8.0 all-to-all-start.1
  153.7 0.0 all-reduce.2.cloned.1.call-start
  153.7 0.6 dynamic_slice.3
  155.0 4.6 fusion.39
  159.6 3.9 copy.97
  163.6 0.0 copy-start.3
  163.6 4.0 copy.98
  167.5 0.0 copy-done.3
  167.5 0.0 copy-done.5
  167.6 0.3 fusion.43
  167.8 0.1 fusion.33
  167.9 2.1 fusion.41
  170.0 0.8 copy-done
  170.8 0.2 fusion.10
  171.0 33.6 %all-to-all-done.1 = bf16[128,4,2048]{2,1,0:T(4,128)(2,1)S(1)} async-done(((bf16[128,4,2048]{2,1,0:T(4,128)(2,1)}), bf16[128,4,2048]{2,1,0:T(4,128)(2,1)S(1)}, u32[]{:S(2)}, u32[]{:S(2)}) %all-to-all-start.1) | async-done | bytes 2097184 | tf_op jit(solution)/shard_map/all_to_all | solution.py:70
  204.6 2.1 reshape.83
  206.7 3.0 fusion.40
  209.7 1.5 copy.76
  211.2 0.9 fusion.42
  212.1 0.8 fusion.16
  212.9 348.0 %pmax.7 = f32[8,2,8]{2,1,0:T(2,128)S(1)} all-reduce(f32[8,2,8]{2,1,0:T(2,128)S(1)} %max.15), channel_id=1, replica_groups=mesh['req'=2,'seq'=128] {'seq'}, use_global_device_ids=true, to_apply=%region_5.6 | all-reduce | flops 128 | bytes 1024 | tf_op jit(solution)/shard_map/pmax | solution.py:76
  560.9 347.7 %psum.15 = f32[8,2,8]{2,1,0:T(2,128)S(1)} all-reduce(f32[8,2,8]{2,1,0:T(2,128)S(1)} %bitcast.104), channel_id=1, replica_groups=mesh['req'=2,'seq'=128] {'seq'}, use_global_device_ids=true, to_apply=%region_10.11 | all-reduce | flops 128 | bytes 1024 | tf_op jit(solution)/shard_map/psum | solution.py:78
  908.7 2.3 copy.79
  911.0 0.0 copy-done.1
  911.0 2.4 convolution_multiply_fusion.4
  913.3 0.0 copy-done.2
  913.3 1.7 fusion.6
  915.0 0.0 all-reduce.2.cloned.1.call-update
  915.0 2.0 reshape_reshape.3
  917.1 199.3 %all-reduce.2.cloned.1.call-done = f32[8,2,8,128]{3,2,1,0:T(8,128)} async-done(((f32[8,2,8,128]{3,2,1,0:T(8,128)}), f32[8,2,8,128]{3,2,1,0:T(8,128)}) %all-reduce.2.cloned.1.call-update) | async-done | bytes 65552 | tf_op jit(solution)/shard_map/psum | solution.py:78
  1116.3 1.1 fusion.8
  1117.4 0.6 copy.122
  (12 shorter events, 0.1 us)
Async XLA Ops:
  19.9 16.0 %copy-start.4 = (s32[256]{0:T(256)S(1)}, s32[256]{0:T(256)}, u32[]{:S(2)}) copy-start(s32[256]{0:T(256)} %param.12) | copy-start | bytes 3076
  19.9 16.3 %copy-start.6 = (s32[32]{0:T(128)S(1)}, s32[32]{0:T(128)}, u32[]{:S(2)}) copy-start(s32[32]{0:T(128)} %param.13) | copy-start | bytes 388
  19.9 112.2 %all-to-all-start = ((bf16[2,128,4,2048]{3,2,0,1:T(4,128)(2,1)}), bf16[2,128,4,2048]{3,2,0,1:T(4,128)(2,1)}, u32[]{:S(2)}, u32[]{:S(2)}) async-start(bf16[2,128,4,2048]{3,2,0,1:T(4,128)(2,1)} %copy.73), calls=%async_computation | async-start | bytes 8388608 | tf_op jit(solution)/shard_map/all_to_all | solution.py:55
  145.7 58.9 %all-to-all-start.1 = ((bf16[128,4,2048]{2,1,0:T(4,128)(2,1)}), bf16[128,4,2048]{2,1,0:T(4,128)(2,1)S(1)}, u32[]{:S(2)}, u32[]{:S(2)}) async-start(bf16[128,4,2048]{2,1,0:T(4,128)(2,1)} %broadcast_select_fusion), calls=%async_computation.1 | async-start | bytes 4194304 | tf_op jit(solution)/shard_map/all_to_all | solution.py:70
  153.7 962.7 %all-reduce.2.cloned.1.call-start = ((), (), s32[]{:S(2)}) async-start(), calls=%async_computation.2 | async-start | bytes 131072 | tf_op jit(solution)/shard_map/psum | solution.py:78
  163.6 4.0 copy-start.3
  163.6 4.0 copy-start.5
  170.0 0.8 copy-start
  212.1 698.9 %copy-start.1 = (f32[8,2,8,1024]{3,2,1,0:T(8,128)S(1)}, f32[8,2,8,1024]{3,2,1,0:T(8,128)}, u32[]{:S(2)}) copy-start(f32[8,2,8,1024]{3,2,1,0:T(8,128)} %copy-done) | copy-start | bytes 1572868
  911.0 2.4 copy-start.2
Sparse Core Ops, SparseCore 0:
  915.1 201.1 all-reduce.1
where the time goes:
time: 1130 us; the launch traced here: 1120 us
  blocking collectives  696 us (62%)
  waiting for transfers between devices  327 us (29%)
  local copies, waits for them, and re-layouts  49.6 us (4%)
  starting transfers between devices  24.1 us (2%)
  between operations  14.8 us (1%)
    pmax x1, blocking collectives, shards(): highest = lax.pmax(partial_value[0], 'seq')  348 us
    psum x1, blocking collectives, shards(): lax.psum((partial_value[1] * factor, partial_value[2] * factor[..., None]...  348 us
    psum x1, waiting for transfers between devices, shards(): lax.psum((partial_value[1] * factor, partial_value[2] * factor[..., None]...  199 us
    all_to_all x1, waiting for transfers between devices, shards(): lax.all_to_all(span_rows.reshape(slot_count, devices, piece_rows, feature...  94.5 us
    all_to_all x1, waiting for transfers between devices, shards(): lax.all_to_all(outgoing, 'seq', split_axis=0, concat_axis=0, tiled=True)  33.6 us
  transfers between devices with their start and end apart: 3, of which 3 were waited for; matrix products, arithmetic and copies ran while one was open for 2% of the time, Pallas kernels for 0%

commit v1 on v0

v1 whole, which is shorter than its diff:
```python
import functools

import jax
import jax.numpy as jnp
from jax import lax
from jax.experimental import pallas as pl
from jax.experimental.pallas import tpu as pltpu
from jax.sharding import PartitionSpec as P

HEAD_DIM = 128
KV_HEADS = 8
TILE_ROWS = 8
NEGATIVE = -(2.0**99)


def halves(value):
    high = value.astype(jnp.bfloat16).astype(jnp.float32)
    low = (value - high).astype(jnp.bfloat16).astype(jnp.float32)
    return high, low


def attention_kernel(
    cache_tiles, span_tiles, live_ref, queries_ref, cache_ref, span_ref, new_ref, out_ref, blocks, total, stats
):
    step = pl.program_id(0)
    lanes = queries_ref.shape[0]
    per_head = lanes // KV_HEADS

    @pl.when(step == 0)
    def _():
        owner = lax.broadcasted_iota(jnp.int32, (lanes, HEAD_DIM), 0) // per_head
        queries = queries_ref[...].astype(jnp.float32)
        for head in range(KV_HEADS):
            blocks[:, head * HEAD_DIM : (head + 1) * HEAD_DIM] = jnp.where(owner == head, queries, 0.0).astype(
                jnp.bfloat16
            )
        total[...] = jnp.zeros_like(total)
        stats[0:1, :] = jnp.full((1, lanes), NEGATIVE, jnp.float32)
        stats[1:2, :] = jnp.zeros((1, lanes), jnp.float32)

    def add(rows_ref, usable):
        half = rows_ref.shape[-1] // 2
        scores = lax.dot_general(
            rows_ref[:, :half], blocks[...], (((1,), (1,)), ((), ())), preferred_element_type=jnp.float32
        )
        scores = jnp.where(usable, scores * HEAD_DIM**-0.5, NEGATIVE)
        before = stats[0:1, :]
        highest = jnp.maximum(before, jnp.max(scores, axis=0, keepdims=True))
        weights = jnp.where(usable, jnp.exp(scores - highest), 0.0)
        scale = jnp.exp(before - highest)
        stats[0:1, :] = highest
        stats[1:2, :] = stats[1:2, :] * scale + jnp.sum(weights, axis=0, keepdims=True)
        product = lax.dot_general(
            weights.astype(jnp.bfloat16),
            rows_ref[:, half:],
            (((0,), (0,)), ((), ())),
            preferred_element_type=jnp.float32,
        )
        own = jnp.concatenate(
            [
                product[head * per_head : (head + 1) * per_head, head * HEAD_DIM : (head + 1) * HEAD_DIM]
                for head in range(KV_HEADS)
            ],
            axis=0,
        )
        column = jnp.transpose(jnp.broadcast_to(scale, (lanes, lanes)))
        total[...] = total[...] * column + own

    def rows_below(count, rows):
        return lax.broadcasted_iota(jnp.int32, (rows, lanes), 0) < count

    @pl.when(step < cache_tiles)
    def _():
        rows = cache_ref.shape[0]
        add(cache_ref, rows_below(live_ref[0] - step * rows, rows))

    for tile in range(span_tiles):

        @pl.when(step == cache_tiles + tile)
        def _(tile=tile):
            rows = span_ref.shape[0]
            add(span_ref, rows_below(live_ref[1 + tile] * rows, rows))

    @pl.when(step == cache_tiles + span_tiles - 1)
    def _():
        rows = new_ref.shape[0]
        row = lax.broadcasted_iota(jnp.int32, (rows, lanes), 0)
        seen = (lax.broadcasted_iota(jnp.int32, (rows, lanes), 1) % per_head) // (per_head // 2)
        add(new_ref, row <= jnp.where(live_ref[1 + span_tiles] > 0, seen, -1))

        high, low = halves(stats[0:1, :])
        scale = jnp.exp(stats[0:1, :] - (high + low))
        sum_high, sum_low = halves(stats[1:2, :] * scale)
        rows4 = jnp.concatenate(
            [high, low, sum_high, sum_low, jnp.zeros((lanes - 4, lanes), jnp.float32)], axis=0
        )
        by_head = jnp.transpose(rows4)
        value_high, value_low = halves(total[...] * jnp.transpose(jnp.broadcast_to(scale, (lanes, lanes))))
        place = lax.broadcasted_iota(jnp.int32, out_ref.shape, 1)
        tiles = jnp.where(place == 0, value_high[:, None, :], 0.0)
        tiles = jnp.where(place == 1, value_low[:, None, :], tiles)
        tiles = jnp.where(place == 2, by_head[:, None, :], tiles)
        out_ref[...] = tiles.astype(jnp.bfloat16)


def attend(live, queries, cache_rows, span_rows, new_rows):
    block = span_rows.shape[0] // 2
    cache_tiles = cache_rows.shape[0] // block
    span_tiles = span_rows.shape[0] // block
    features = cache_rows.shape[1]
    lanes = queries.shape[0]
    return pl.pallas_call(
        functools.partial(attention_kernel, cache_tiles, span_tiles),
        grid=(cache_tiles + span_tiles,),
        in_specs=[
            pl.BlockSpec(memory_space=pltpu.SMEM),
            pl.BlockSpec((lanes, HEAD_DIM), lambda i: (0, 0)),
            pl.BlockSpec((block, features), lambda i: (jnp.minimum(i, cache_tiles - 1), 0)),
            pl.BlockSpec((block, features), lambda i: (jnp.maximum(i - cache_tiles, 0), 0)),
            pl.BlockSpec(new_rows.shape, lambda i: (0, 0)),
        ],
        out_specs=pl.BlockSpec((lanes, TILE_ROWS, HEAD_DIM), lambda i: (0, 0, 0)),
        out_shape=jax.ShapeDtypeStruct((lanes, TILE_ROWS, HEAD_DIM), jnp.bfloat16),
        scratch_shapes=[
            pltpu.VMEM((lanes, KV_HEADS * HEAD_DIM), jnp.bfloat16),
            pltpu.VMEM((lanes, HEAD_DIM), jnp.float32),
            pltpu.VMEM((8, lanes), jnp.float32),
        ],
        compiler_params=pltpu.CompilerParams(vmem_limit_bytes=40 * 2**20),
        cost_estimate=pl.CostEstimate(flops=2**31, bytes_accessed=2**23, transcendentals=2**18),
    )(live, queries, cache_rows, span_rows, new_rows)


def deal_kernel(count, own_pieces, route_ref, arrived_ref, out_ref, partial, sems):
    whole = pltpu.make_async_copy(arrived_ref.at[:, own_pieces], partial, sems.at[count])
    whole.start()
    out_ref[...] = jnp.zeros_like(out_ref)
    pieces = out_ref.shape[1] - 1

    def block_copy(number):
        return pltpu.make_async_copy(
            arrived_ref.at[route_ref[1, number], pl.ds(route_ref[2, number] * pieces, pieces)],
            out_ref.at[route_ref[0, number], pl.ds(0, pieces)],
            sems.at[number],
        )

    for number in range(count):
        block_copy(number).start()
    whole.wait()
    tiles = partial[...].astype(jnp.float32)
    row = lax.broadcasted_iota(jnp.int32, tiles.shape, 1)
    lane = lax.broadcasted_iota(jnp.int32, tiles.shape, 2)
    highest = jnp.sum(jnp.where((row == 2) & (lane < 2), tiles, 0.0), axis=(1, 2), keepdims=True)
    factor = jnp.exp(highest - jnp.max(highest, axis=0, keepdims=True))
    merged = jnp.sum(tiles * factor, axis=0)
    row = lax.broadcasted_iota(jnp.int32, merged.shape, 0)
    lane = lax.broadcasted_iota(jnp.int32, merged.shape, 1)
    weight = jnp.sum(jnp.where((row == 2) & ((lane == 2) | (lane == 3)), merged, 0.0), axis=(0, 1), keepdims=True)
    value = jnp.sum(jnp.where(row < 2, merged, 0.0), axis=0, keepdims=True) / weight
    result = jnp.broadcast_to(value, merged.shape).astype(out_ref.dtype)
    out_ref[:, pieces] = jnp.broadcast_to(result[None], (out_ref.shape[0],) + result.shape)
    for number in range(count):
        block_copy(number).wait()


def deal(route, arrived, pieces):
    devices = arrived.shape[0]
    count = route.shape[1]
    return pl.pallas_call(
        functools.partial(deal_kernel, count, arrived.shape[1] - 1),
        in_specs=[pl.BlockSpec(memory_space=pltpu.SMEM), pl.BlockSpec(memory_space=pl.ANY)],
        out_specs=pl.BlockSpec(memory_space=pltpu.VMEM),
        out_shape=jax.ShapeDtypeStruct((devices, pieces + 1) + arrived.shape[2:], arrived.dtype),
        scratch_shapes=[
            pltpu.VMEM((devices,) + arrived.shape[2:], arrived.dtype),
            pltpu.SemaphoreType.DMA((count + 1,)),
        ],
        compiler_params=pltpu.CompilerParams(vmem_limit_bytes=40 * 2**20),
        cost_estimate=pl.CostEstimate(flops=2**20, bytes_accessed=2**22, transcendentals=2**8),
    )(route, arrived)


def shards(queries, new_tokens, cache_rows, cache_length, span_rows, slot_blocks, decode_owner):
    devices = lax.axis_size("seq")
    own_index = lax.axis_index("seq")
    slot_count, block_rows, features = span_rows.shape
    step_count = queries.shape[0]
    group = queries.shape[1] // (KV_HEADS * HEAD_DIM)
    pieces = block_rows * features // (devices * TILE_ROWS * HEAD_DIM)
    parts = features // (pieces * HEAD_DIM)

    grouped = queries.reshape(step_count, KV_HEADS, group, HEAD_DIM).transpose(1, 0, 2, 3).reshape(-1, HEAD_DIM)
    own_slots = lax.dynamic_slice_in_dim(slot_blocks, own_index * slot_count, slot_count)
    live = jnp.concatenate(
        [
            jnp.clip(cache_length - own_index * cache_rows.shape[0], 0, cache_rows.shape[0]),
            (own_slots >= 0).astype(jnp.int32),
            (own_index == 0).astype(jnp.int32)[None],
        ]
    )
    new_rows = jnp.pad(new_tokens, ((0, 16 - step_count), (0, 0)))
    partial = attend(live, grouped, cache_rows, span_rows.reshape(-1, features), new_rows)

    shares = span_rows.reshape(slot_count, devices // parts, TILE_ROWS, parts, pieces, HEAD_DIM)
    shares = shares.transpose(1, 3, 0, 4, 2, 5).reshape(devices, slot_count * pieces, TILE_ROWS, HEAD_DIM)
    arrived = lax.all_to_all(jnp.concatenate([shares, partial[:, None]], axis=1), "seq", 0, 0, tiled=True)

    numbers = jnp.arange(decode_owner.shape[0], dtype=jnp.int32)
    holder = jnp.argmax(slot_blocks[None, :] == numbers[:, None], axis=1).astype(jnp.int32)
    route = jnp.stack([decode_owner, holder // slot_count, holder % slot_count])
    dealt = lax.all_to_all(deal(route, arrived, pieces), "seq", 0, 0, tiled=True)

    relaid = dealt[:, :pieces].reshape(devices // parts, parts, pieces, TILE_ROWS, HEAD_DIM)
    relaid = relaid.transpose(0, 3, 1, 2, 4).reshape(1, block_rows, features)
    result = dealt[:, pieces, 0].reshape(KV_HEADS, step_count, group * HEAD_DIM)
    attention = result.transpose(1, 0, 2).reshape(step_count, -1)
    return (attention, relaid)


def solution(mesh):
    placed = (
        P("req", None),
        P("req", None),
        P(("req", "seq"), None),
        P("req"),
        P(("req", "seq"), None, None),
        P("req"),
        P("req"),
    )
    return jax.shard_map(
        shards,
        mesh=mesh,
        in_specs=placed,
        out_specs=(P("req", None), P(("req", "seq"), None, None)),
        check_vma=False,
    )
```

time: 1130 us -> 208 us (0.18)
  blocking collectives: 696 us -> 64.3 us
  waiting for transfers between devices: 327 us -> 101 us
  local copies, waits for them, and re-layouts: 49.6 us -> 13.1 us
  between operations: 14.8 us -> 1.36 us
    pmax x1 -> x0, blocking collectives: 348 us -> none  [shards(): highest = lax.pmax(partial_value[0], 'seq')]
    psum x1 -> x0, blocking collectives: 348 us -> none  [shards(): lax.psum((partial_value[1] * factor, partial_value[2] * factor[..., None]...]
    psum x1 -> x0, waiting for transfers between devices: 199 us -> none  [shards(): lax.psum((partial_value[1] * factor, partial_value[2] * factor[..., None]...]
    all_to_all x0 -> x1, blocking collectives: none -> 64.3 us  [shards(): lax.all_to_all(deal(route, arrived, pieces), 'seq', 0, 0, tiled=True)]
    all_to_all x2 -> x1, waiting for transfers between devices: 128 us -> 101 us  [shards(): lax.all_to_all(jnp.concatenate([shares, partial[:, None]], axis=1), 'seq'...]
    all_to_all x2 -> x1, starting transfers between devices: 24 us -> 16 us  [shards(): lax.all_to_all(jnp.concatenate([shares, partial[:, None]], axis=1), 'seq'...]
  transfers between devices with their start and end apart: 3 -> 1, of which waited for: 3 -> 1; matrix products, arithmetic and copies ran while one was open for 2% -> 0% of each run, Pallas kernels for 0% -> 0%
where the time goes in v1:
time: 208 us
  waiting for transfers between devices  101 us (49%)
  blocking collectives  64.3 us (31%)
  starting transfers between devices  16 us (8%)
  local copies, waits for them, and re-layouts  13.1 us (6%)
  Pallas kernels  8.25 us (4%)
  other arithmetic  3.33 us (2%)
    all_to_all x1, waiting for transfers between devices, shards(): lax.all_to_all(jnp.concatenate([shares, partial[:, None]], axis=1), 'seq'...  101 us
    all_to_all x1, blocking collectives, shards(): lax.all_to_all(deal(route, arrived, pieces), 'seq', 0, 0, tiled=True)  64.3 us
    all_to_all x1, starting transfers between devices, shards(): lax.all_to_all(jnp.concatenate([shares, partial[:, None]], axis=1), 'seq'...  16 us
    pallas_call x1, Pallas kernels, attend(): pl.pallas_call(functools.partial(attention_kernel, cache_tiles, span_tile...  5.56 us
    reshape x1, local copies, waits for them, and re-layouts, shards(): span_rows.reshape(slot_count, devices // parts, TILE_ROWS, parts, pieces,...  5.5 us
    unnamed x13, local copies, waits for them, and re-layouts  5.16 us
  transfers between devices with their start and end apart: 1, of which 1 were waited for; matrix products, arithmetic and copies ran while one was open for 0% of the time, Pallas kernels for 0%

profile of v1, /device:TPU:2, one launch (start us, length us, event | category | flops | bytes accessed | tf_op | source)
XLA Modules:
  0.0 207.5 jit_solution(2968791242628170884)
XLA Ops:
  1.3 0.8 copy.18
  2.1 0.0 copy-start.4
  2.1 0.0 copy-start.3
  2.1 5.5 %copy.14 = bf16[2,64,8,2,8,128]{5,2,4,0,3,1:T(8,128)(2,1)} copy(bf16[2,64,8,2,8,128]{5,2,4,3,1,0:T(8,128)(2,1)} %bitcast.29) | data formatting | bytes 8388608 | tf_op jit(solution)/shard_map/reshape | solution.py:204
  7.6 0.0 copy-done.4
  7.6 0.1 compare_convert_fusion
  7.7 0.0 copy-done.3
  7.7 0.1 pad_add_fusion.1.live_ref
  7.8 0.0 copy-start
  7.8 2.2 %copy-done = bf16[2,512,2048]{2,1,0:T(8,128)(2,1)S(1)} copy-done((bf16[2,512,2048]{2,1,0:T(8,128)(2,1)S(1)}, bf16[2,512,2048]{2,1,0:T(8,128)(2,1)}, u32[]{:S(2)}) %copy-start) | copy-done | bytes 4194328
  9.9 0.0 copy-start.1
  9.9 2.2 %copy-done.1 = bf16[1024,2048]{1,0:T(8,128)(2,1)S(1)} copy-done((bf16[1024,2048]{1,0:T(8,128)(2,1)S(1)}, bf16[1024,2048]{1,0:T(8,128)(2,1)}, u32[]{:S(2)}) %copy-start.1) | copy-done | bytes 4194328
  12.1 0.0 copy-start.2
  12.1 5.6 %shard_map.86 = bf16[128,8,128]{2,1,0:T(8,128)(2,1)S(1)} custom-call(s32[4]{0:T(128)S(1)} %pad_add_fusion.1.live_ref, bf16[128,128]{1,0:T(8,128)(2,1)S(1)} %bitcast.32, bf16[1024,2048]{1,0:T(8,128)(2,1)S(1)} %copy-done.1, bf16[1024,2048]{1,0:T(8,128)(2,1)S(1)} %bitcast.30, bf16[16,2048]{1,0:T(8,128)(2,1)S(1)} %pad.4.new_ref), custom_call_target="tpu_custom_call" | custom-call | flops 2147483648 | bytes 8388608 | tf_op jit(solution)/shard_map/pallas_call | solution.py:112
  17.7 0.0 copy-done.2
  17.7 2.5 %pad_maximum_fusion = bf16[128,17,8,128]{3,2,1,0:T(8,128)(2,1)} fusion(bf16[128,1,8,128]{3,2,1,0:T(8,128)(2,1)S(1)} %bitcast.31, bf16[128,16,8,128]{3,2,1,0:T(8,128)(2,1)S(1)} %bitcast.33), kind=kLoop, calls=%fused_computation | loop fusion | flops 2228224 | bytes 8912896 | tf_op jit(solution)/shard_map/concatenate | solution.py:206
  20.2 0.0 copy-start.5
  20.2 16.0 %all-to-all-start = ((bf16[128,17,8,128]{3,2,1,0:T(8,128)(2,1)}), bf16[128,17,8,128]{3,2,1,0:T(8,128)(2,1)}, u32[]{:S(2)}, u32[]{:S(2)}) async-start(bf16[128,17,8,128]{3,2,1,0:T(8,128)(2,1)} %pad_maximum_fusion), calls=%async_computation | async-start | bytes 8912896 | tf_op jit(solution)/shard_map/all_to_all | solution.py:206
  36.2 0.6 iota_reduce_fusion
  36.8 0.0 copy-done.5
  36.9 101.2 %all-to-all-done.arrived_ref = bf16[128,17,8,128]{3,2,1,0:T(8,128)(2,1)} async-done(((bf16[128,17,8,128]{3,2,1,0:T(8,128)(2,1)}), bf16[128,17,8,128]{3,2,1,0:T(8,128)(2,1)}, u32[]{:S(2)}, u32[]{:S(2)}) %all-to-all-start) | async-done | bytes 4456480 | tf_op jit(solution)/shard_map/all_to_all | solution.py:206
  138.1 2.7 %shard_map.87 = bf16[128,9,8,128]{3,2,1,0:T(8,128)(2,1)S(1)} custom-call(s32[3,32]{1,0:T(4,128)S(1)} %pad_add_fusion.route_ref, bf16[128,17,8,128]{3,2,1,0:T(8,128)(2,1)} %all-to-all-done.arrived_ref), custom_call_target="tpu_custom_call" | custom-call | flops 1048576 | bytes 4194304 | tf_op jit(solution)/shard_map/pallas_call | solution.py:169
  140.8 64.3 %all_to_all.10 = bf16[128,9,8,128]{3,2,1,0:T(8,128)(2,1)S(1)} all-to-all(bf16[128,9,8,128]{3,2,1,0:T(8,128)(2,1)S(1)} %shard_map.87), channel_id=1, replica_groups=mesh['req'=2,'seq'=128] {'seq'}, dimensions={0} | all-to-all | bytes 4718592 | tf_op jit(solution)/shard_map/all_to_all | solution.py:211
  205.1 0.2 slice_reduce_fusion
  205.3 0.6 reshape_squeeze.3
  205.9 1.6 slice.9
  (4 shorter events, 0.0 us)
Async XLA Ops:
  2.1 5.5 %copy-start.4 = (s32[256]{0:T(256)S(1)}, s32[256]{0:T(256)}, u32[]{:S(2)}) copy-start(s32[256]{0:T(256)} %param.12) | copy-start | bytes 3076
  2.1 5.6 %copy-start.3 = (bf16[2,2048]{1,0:T(2,128)(2,1)S(1)}, bf16[2,2048]{1,0:T(2,128)(2,1)}, u32[]{:S(2)}) copy-start(bf16[2,2048]{1,0:T(2,128)(2,1)} %param.8) | copy-start | bytes 24580
  7.8 2.2 %copy-start = (bf16[2,512,2048]{2,1,0:T(8,128)(2,1)S(1)}, bf16[2,512,2048]{2,1,0:T(8,128)(2,1)}, u32[]{:S(2)}) copy-start(bf16[2,512,2048]{2,1,0:T(8,128)(2,1)} %param.11) | copy-start | bytes 12582916
  9.9 2.2 %copy-start.1 = (bf16[1024,2048]{1,0:T(8,128)(2,1)S(1)}, bf16[1024,2048]{1,0:T(8,128)(2,1)}, u32[]{:S(2)}) copy-start(bf16[1024,2048]{1,0:T(8,128)(2,1)} %cache_ref.1) | copy-start | bytes 12582916
  12.1 5.6 %copy-start.2 = (bf16[2,64,8,2,8,128]{5,2,4,0,3,1:T(8,128)(2,1)S(1)}, bf16[2,64,8,2,8,128]{5,2,4,0,3,1:T(8,128)(2,1)}, u32[]{:S(2)}) copy-start(bf16[2,64,8,2,8,128]{5,2,4,0,3,1:T(8,128)(2,1)} %copy.14) | copy-start | bytes 12582916
  20.2 16.6 %copy-start.5 = (s32[32]{0:T(128)S(1)}, s32[32]{0:T(128)}, u32[]{:S(2)}) copy-start(s32[32]{0:T(128)} %param.13) | copy-start | bytes 388
  20.2 117.9 %all-to-all-start = ((bf16[128,17,8,128]{3,2,1,0:T(8,128)(2,1)}), bf16[128,17,8,128]{3,2,1,0:T(8,128)(2,1)}, u32[]{:S(2)}, u32[]{:S(2)}) async-start(bf16[128,17,8,128]{3,2,1,0:T(8,128)(2,1)} %pad_maximum_fusion), calls=%async_computation | async-start | bytes 8912896 | tf_op jit(solution)/shard_map/all_to_all | solution.py:206

commit v2 on v1

v2 whole, which is shorter than its diff:
```python
import functools

import jax
import jax.numpy as jnp
from jax import lax
from jax.experimental import pallas as pl
from jax.experimental.pallas import tpu as pltpu
from jax.sharding import PartitionSpec as P

HEAD_DIM = 128
KV_HEADS = 8
NEGATIVE = -(2.0**99)

PLANE_X = 4
PLANE_Y = 4
PAIR = 2
CLUSTERS = 4
CLUSTER = PLANE_Y * PAIR * PLANE_X
RUN = PAIR * PLANE_X
CAPACITIES = (4, 5, 6, 8, 32)
VMEM_LIMIT = 56 * 2**20


def device_at(cluster, position):
    return (position // RUN) * RUN * CLUSTERS + cluster * RUN + position % RUN


def cluster_of(device):
    return (device // RUN) % CLUSTERS


def position_of(device):
    return (device // (RUN * CLUSTERS)) * RUN + device % RUN


def halves(value):
    high = value.astype(jnp.bfloat16).astype(jnp.float32)
    low = (value - high).astype(jnp.bfloat16).astype(jnp.float32)
    return high, low


def packed(value, highest, total):
    shape = (value.shape[0], 8, HEAD_DIM)
    row = lax.broadcasted_iota(jnp.int32, shape, 1)
    lane = lax.broadcasted_iota(jnp.int32, shape, 2)
    value_high, value_low = halves(value)
    numbers = jnp.zeros(shape, jnp.float32)
    for place, part in enumerate(halves(highest) + halves(total)):
        numbers = jnp.where(lane == place, part, numbers)
    tiles = jnp.where(row == 2, numbers, 0.0)
    tiles = jnp.where(row == 0, value_high, tiles)
    return jnp.where(row == 1, value_low, tiles)


def merged(tiles):
    row = lax.broadcasted_iota(jnp.int32, tiles.shape, 2)
    lane = lax.broadcasted_iota(jnp.int32, tiles.shape, 3)
    each = jnp.sum(jnp.where((row == 2) & (lane < 2), tiles, 0.0), axis=(2, 3), keepdims=True)
    highest = jnp.max(each, axis=0, keepdims=True)
    summed = jnp.sum(tiles * jnp.exp(each - highest), axis=0)
    row = lax.broadcasted_iota(jnp.int32, summed.shape, 1)
    lane = lax.broadcasted_iota(jnp.int32, summed.shape, 2)
    value = jnp.sum(jnp.where(row < 2, summed, 0.0), axis=1, keepdims=True)
    total = jnp.sum(
        jnp.where((row == 2) & ((lane == 2) | (lane == 3)), summed, 0.0), axis=(1, 2), keepdims=True
    )
    return value, highest[0], total


def attention_kernel(
    cache_tiles, span_tiles, live_ref, queries_ref, cache_ref, span_ref, new_ref, out_ref, blocks, total, stats
):
    step = pl.program_id(0)
    lanes = queries_ref.shape[0]
    per_head = lanes // KV_HEADS

    @pl.when(step == 0)
    def _():
        owner = lax.broadcasted_iota(jnp.int32, (lanes, HEAD_DIM), 0) // per_head
        queries = queries_ref[...].astype(jnp.float32)
        for head in range(KV_HEADS):
            blocks[:, head * HEAD_DIM : (head + 1) * HEAD_DIM] = jnp.where(owner == head, queries, 0.0).astype(
                jnp.bfloat16
            )
        total[...] = jnp.zeros_like(total)
        stats[0:1, :] = jnp.full((1, lanes), NEGATIVE, jnp.float32)
        stats[1:2, :] = jnp.zeros((1, lanes), jnp.float32)

    def add(rows_ref, usable):
        half = rows_ref.shape[-1] // 2
        scores = lax.dot_general(
            rows_ref[:, :half], blocks[...], (((1,), (1,)), ((), ())), preferred_element_type=jnp.float32
        )
        scores = jnp.where(usable, scores * HEAD_DIM**-0.5, NEGATIVE)
        before = stats[0:1, :]
        highest = jnp.maximum(before, jnp.max(scores, axis=0, keepdims=True))
        weights = jnp.where(usable, jnp.exp(scores - highest), 0.0)
        scale = jnp.exp(before - highest)
        stats[0:1, :] = highest
        stats[1:2, :] = stats[1:2, :] * scale + jnp.sum(weights, axis=0, keepdims=True)
        product = lax.dot_general(
            weights.astype(jnp.bfloat16),
            rows_ref[:, half:],
            (((0,), (0,)), ((), ())),
            preferred_element_type=jnp.float32,
        )
        own = jnp.concatenate(
            [
                product[head * per_head : (head + 1) * per_head, head * HEAD_DIM : (head + 1) * HEAD_DIM]
                for head in range(KV_HEADS)
            ],
            axis=0,
        )
        column = jnp.transpose(jnp.broadcast_to(scale, (lanes, lanes)))
        total[...] = total[...] * column + own

    def rows_below(count, rows):
        return lax.broadcasted_iota(jnp.int32, (rows, lanes), 0) < count

    @pl.when(step < cache_tiles)
    def _():
        rows = cache_ref.shape[0]
        add(cache_ref, rows_below(live_ref[0] - step * rows, rows))

    for tile in range(span_tiles):

        @pl.when(step == cache_tiles + tile)
        def _(tile=tile):
            rows, features = span_ref.shape
            share = rows // out_ref.shape[0]
            out_ref[:, tile * share : (tile + 1) * share, :features] = span_ref[...].reshape(-1, share, features)
            add(span_ref, rows_below(live_ref[1 + tile] * rows, rows))

    @pl.when(step == cache_tiles + span_tiles - 1)
    def _():
        rows, features = new_ref.shape
        row = lax.broadcasted_iota(jnp.int32, (rows, lanes), 0)
        seen = (lax.broadcasted_iota(jnp.int32, (rows, lanes), 1) % per_head) // (per_head // 2)
        add(new_ref, row <= jnp.where(live_ref[1 + span_tiles] > 0, seen, -1))

        high, low = halves(stats[0:1, :])
        scale = jnp.exp(stats[0:1, :] - (high + low))
        by_head = jnp.transpose(
            jnp.concatenate(
                [high + low, stats[1:2, :] * scale, scale, jnp.zeros((lanes - 3, lanes), jnp.float32)], axis=0
            )
        )
        value = total[...] * by_head[:, 2:3]
        tiles = packed(value[:, None, :], by_head[:, None, 0:1], by_head[:, None, 1:2])
        count = out_ref.shape[0]
        out_ref[:, :, features:] = tiles.reshape(count, -1, HEAD_DIM).astype(jnp.bfloat16)


def attend(live, queries, cache_rows, span_rows, new_rows):
    block = span_rows.shape[0] // 2
    cache_tiles = cache_rows.shape[0] // block
    span_tiles = span_rows.shape[0] // block
    features = cache_rows.shape[1]
    lanes = queries.shape[0]
    shape = (CLUSTER, span_rows.shape[0] // CLUSTER, features + HEAD_DIM)
    return pl.pallas_call(
        functools.partial(attention_kernel, cache_tiles, span_tiles),
        grid=(cache_tiles + span_tiles,),
        in_specs=[
            pl.BlockSpec(memory_space=pltpu.SMEM),
            pl.BlockSpec((lanes, HEAD_DIM), lambda i: (0, 0)),
            pl.BlockSpec((block, features), lambda i: (jnp.minimum(i, cache_tiles - 1), 0)),
            pl.BlockSpec((block, features), lambda i: (jnp.maximum(i - cache_tiles, 0), 0)),
            pl.BlockSpec(new_rows.shape, lambda i: (0, 0)),
        ],
        out_specs=pl.BlockSpec(shape, lambda i: (0, 0, 0)),
        out_shape=jax.ShapeDtypeStruct(shape, jnp.bfloat16),
        scratch_shapes=[
            pltpu.VMEM((lanes, KV_HEADS * HEAD_DIM), jnp.bfloat16),
            pltpu.VMEM((lanes, HEAD_DIM), jnp.float32),
            pltpu.VMEM((8, lanes), jnp.float32),
        ],
        compiler_params=pltpu.CompilerParams(vmem_limit_bytes=VMEM_LIMIT),
        cost_estimate=pl.CostEstimate(flops=2**31, bytes_accessed=2**23, transcendentals=2**18),
    )(live, queries, cache_rows, span_rows, new_rows)


def outgoing_kernel(route_ref, arrived_ref, *refs):
    out_refs, (partial, sems) = refs[:-2], refs[-2:]
    count = route_ref.shape[1]
    features = arrived_ref.shape[-1] - HEAD_DIM
    share = arrived_ref.shape[1] // 2
    whole = pltpu.make_async_copy(arrived_ref.at[:, :, pl.ds(features, HEAD_DIM)], partial, sems.at[count])
    whole.start()

    def each(act):
        for number in range(count):
            source = arrived_ref.at[
                route_ref[1, number], pl.ds(route_ref[2, number] * share, share), pl.ds(0, features)
            ]
            for distance in range(1, CLUSTERS):

                @pl.when((route_ref[0, number] > 0) & (route_ref[3, number] == distance))
                def _(source=source, number=number, distance=distance):
                    target = out_refs[distance - 1].at[
                        pl.ds(route_ref[4, number] * share, share), pl.ds(0, features)
                    ]
                    act(pltpu.make_async_copy(source, target, sems.at[number]))

    each(lambda copy: copy.start())
    whole.wait()
    tiles = partial[...].astype(jnp.float32).reshape(partial.shape[0], -1, 8, HEAD_DIM)
    result = packed(*merged(tiles)).reshape(-1, HEAD_DIM).astype(jnp.bfloat16)
    for out_ref in out_refs:
        out_ref[: result.shape[0], features:] = result
    each(lambda copy: copy.wait())


def outgoing(capacity, route, arrived):
    share = arrived.shape[1] // 2
    shape = jax.ShapeDtypeStruct((capacity * share, arrived.shape[2]), arrived.dtype)
    return pl.pallas_call(
        outgoing_kernel,
        in_specs=[pl.BlockSpec(memory_space=pltpu.SMEM), pl.BlockSpec(memory_space=pl.ANY)],
        out_specs=[pl.BlockSpec(memory_space=pltpu.VMEM)] * (CLUSTERS - 1),
        out_shape=[shape] * (CLUSTERS - 1),
        scratch_shapes=[
            pltpu.VMEM(arrived.shape[:2] + (HEAD_DIM,), arrived.dtype),
            pltpu.SemaphoreType.DMA((route.shape[1] + 1,)),
        ],
        compiler_params=pltpu.CompilerParams(vmem_limit_bytes=VMEM_LIMIT),
        cost_estimate=pl.CostEstimate(flops=2**20, bytes_accessed=2**21, transcendentals=2**8),
    )(route, arrived)


def dealt_kernel(route_ref, arrived_ref, sent_ref, *refs):
    from_refs, out_ref, partial, sems = refs[: CLUSTERS - 1], refs[-3], refs[-2], refs[-1]
    count = route_ref.shape[1]
    share, width = out_ref.shape[1:]
    features = width - HEAD_DIM
    tile_rows = partial.shape[1]
    partial_refs = (sent_ref,) + from_refs
    partial_copies = [
        pltpu.make_async_copy(
            ref.at[pl.ds(0, tile_rows), pl.ds(features, HEAD_DIM)], partial.at[place], sems.at[count + place]
        )
        for place, ref in enumerate(partial_refs)
    ]
    for copy in partial_copies:
        copy.start()
    out_ref[...] = jnp.zeros_like(out_ref)

    def each(act):
        for number in range(count):
            target = out_ref.at[route_ref[6, number], slice(None), pl.ds(0, features)]
            sources = [
                arrived_ref.at[
                    route_ref[1, number], pl.ds(route_ref[2, number] * share, share), pl.ds(0, features)
                ]
            ] + [ref.at[pl.ds(route_ref[4, number] * share, share), pl.ds(0, features)] for ref in from_refs]
            for distance, source in enumerate(sources):

                @pl.when((route_ref[5, number] > 0) & (route_ref[3, number] == distance))
                def _(source=source, target=target, number=number):
                    act(pltpu.make_async_copy(source, target, sems.at[number]))

    each(lambda copy: copy.start())
    for copy in partial_copies:
        copy.wait()
    tiles = partial[...].astype(jnp.float32).reshape(CLUSTERS, -1, 8, HEAD_DIM)
    value, _, total = merged(tiles)
    result = value / total
    row = lax.broadcasted_iota(jnp.int32, (share, HEAD_DIM), 0)
    rows = jnp.zeros((share, HEAD_DIM), jnp.float32)
    for place in range(result.shape[0]):
        rows = jnp.where(row == place, result[place], rows)
    rows = rows.astype(out_ref.dtype)
    out_ref[:, :, features:] = jnp.broadcast_to(rows[None], (out_ref.shape[0],) + rows.shape)
    each(lambda copy: copy.wait())


def dealt(route, arrived, sent, received):
    share = arrived.shape[1] // 2
    tile_rows = arrived.shape[1]
    return pl.pallas_call(
        dealt_kernel,
        in_specs=[pl.BlockSpec(memory_space=pltpu.SMEM)] + [pl.BlockSpec(memory_space=pl.ANY)] * (2 + len(received)),
        out_specs=pl.BlockSpec(memory_space=pltpu.VMEM),
        out_shape=jax.ShapeDtypeStruct((CLUSTER, share, arrived.shape[2]), arrived.dtype),
        scratch_shapes=[
            pltpu.VMEM((CLUSTERS, tile_rows, HEAD_DIM), arrived.dtype),
            pltpu.SemaphoreType.DMA((route.shape[1] + CLUSTERS,)),
        ],
        compiler_params=pltpu.CompilerParams(vmem_limit_bytes=VMEM_LIMIT),
        cost_estimate=pl.CostEstimate(flops=2**20, bytes_accessed=2**22, transcendentals=2**8),
    )(route, arrived, sent, *received)


def crossed(capacity, route, arrived):
    sent = outgoing(capacity, route, arrived)
    received = [
        lax.ppermute(
            rows,
            "seq",
            [
                (device_at(cluster, position), device_at((cluster + distance) % CLUSTERS, position))
                for cluster in range(CLUSTERS)
                for position in range(CLUSTER)
            ],
        )
        for distance, rows in enumerate(sent, 1)
    ]
    return dealt(route, arrived, sent[0], received)


def shards(queries, new_tokens, cache_rows, cache_length, span_rows, slot_blocks, decode_owner):
    own_index = lax.axis_index("seq")
    slot_count, block_rows, features = span_rows.shape
    step_count = queries.shape[0]
    group = queries.shape[1] // (KV_HEADS * HEAD_DIM)
    count = decode_owner.shape[0]
    clusters = [[device_at(cluster, position) for position in range(CLUSTER)] for cluster in range(CLUSTERS)]

    grouped = queries.reshape(step_count, KV_HEADS, group, HEAD_DIM).transpose(1, 0, 2, 3).reshape(-1, HEAD_DIM)
    own_slots = lax.dynamic_slice_in_dim(slot_blocks, own_index * slot_count, slot_count)
    live = jnp.concatenate(
        [
            jnp.clip(cache_length - own_index * cache_rows.shape[0], 0, cache_rows.shape[0]),
            (own_slots >= 0).astype(jnp.int32),
            (own_index == 0).astype(jnp.int32)[None],
        ]
    )
    new_rows = jnp.pad(new_tokens, ((0, 16 - step_count), (0, 0)))
    shares = attend(live, grouped, cache_rows, span_rows.reshape(-1, features), new_rows)
    arrived = lax.all_to_all(shares, "seq", 0, 0, axis_index_groups=clusters, tiled=True)

    numbers = jnp.arange(count, dtype=jnp.int32)
    slot = jnp.argmax(slot_blocks[None, :] == numbers[:, None], axis=1).astype(jnp.int32)
    holder = slot // slot_count
    source, target = cluster_of(holder), cluster_of(decode_owner)
    distance = (target - source) % CLUSTERS
    journey = source * CLUSTERS + target
    earlier = (journey[None, :] == journey[:, None]) & (numbers[None, :] < numbers[:, None])
    rank = jnp.sum(earlier.astype(jnp.int32), axis=1)
    own_cluster = cluster_of(own_index)
    route = jnp.stack(
        [
            ((source == own_cluster) & (distance > 0)).astype(jnp.int32),
            position_of(holder),
            slot % slot_count,
            distance,
            rank,
            (target == own_cluster).astype(jnp.int32),
            position_of(decode_owner),
            jnp.zeros_like(rank),
        ]
    )
    needed = jnp.max(jnp.where(distance > 0, rank + 1, 0)).reshape(1)
    needed = jnp.maximum(needed, lax.ppermute(needed, "req", [(0, 1), (1, 0)]))
    choice = jnp.sum((needed > jnp.array(CAPACITIES[:-1], jnp.int32)).astype(jnp.int32))
    shares = lax.switch(
        choice, [functools.partial(crossed, capacity) for capacity in CAPACITIES], route, arrived
    )
    arrived = lax.all_to_all(shares, "seq", 0, 0, axis_index_groups=clusters, tiled=True)

    relaid = arrived[:, :, :features].reshape(1, block_rows, features)
    per_device = step_count * KV_HEADS * group // CLUSTER
    result = arrived[:, :per_device, features:].reshape(KV_HEADS, step_count, group * HEAD_DIM)
    attention = result.transpose(1, 0, 2).reshape(step_count, -1)
    return (attention, relaid)


def solution(mesh):
    placed = (
        P("req", None),
        P("req", None),
        P(("req", "seq"), None),
        P("req"),
        P(("req", "seq"), None, None),
        P("req"),
        P("req"),
    )
    return jax.shard_map(
        shards,
        mesh=mesh,
        in_specs=placed,
        out_specs=(P("req", None), P(("req", "seq"), None, None)),
        check_vma=False,
    )
```

time: 208 us -> 169 us (0.81)
  blocking collectives: 64.3 us -> 36.8 us
  waiting for transfers between devices: 101 us -> 80 us
  Pallas kernels: 8.25 us -> 16.9 us
  local copies, waits for them, and re-layouts: 13.1 us -> 9.48 us
  starting transfers between devices: 16 us -> 18.5 us
    all_to_all x1, waiting for transfers between devices: 101 us -> 53.4 us  [shards(): lax.all_to_all(shares, 'seq', 0, 0, axis_index_groups=clusters, tiled=True)]
    all_to_all x1, blocking collectives: 64.3 us -> 36.8 us  [shards(): lax.all_to_all(shares, 'seq', 0, 0, axis_index_groups=clusters, tiled=True)]
    ppermute x0 -> x4, waiting for transfers between devices: none -> 26.7 us  [the longest x3 25.5 us: crossed(): lax.ppermute(rows, 'seq', [(device_at(cluster, position), device_at((clus...]
    ppermute x0 -> x4, starting transfers between devices: none -> 9.3 us  [the longest x3 9.3 us: crossed(): lax.ppermute(rows, 'seq', [(device_at(cluster, position), device_at((clus...]
    all_to_all x1, starting transfers between devices: 16 us -> 9.17 us  [shards(): lax.all_to_all(shares, 'seq', 0, 0, axis_index_groups=clusters, tiled=True)]
    reshape x1 -> x2, local copies, waits for them, and re-layouts: 5.5 us -> 0.03 us  [shards(): arrived[:, :per_device, features:]]
    pallas_call x1, Pallas kernels: 5.56 us -> 10.4 us  [attend(): pl.pallas_call(functools.partial(attention_kernel, cache_tiles, span_tile...]
    pallas_call x1 -> x2, Pallas kernels: 2.69 us -> 6.43 us  [the longest x1 3.72 us: outgoing(): pl.pallas_call(outgoing_kernel, in_specs=[pl.BlockSpec(memory_space=pltpu...]
  transfers between devices with their start and end apart: 1 -> 5, of which waited for: 1 -> 4; matrix products, arithmetic and copies ran while one was open for 0% -> 1% of each run, Pallas kernels for 0% -> 0%
where the time goes in v2:
time: 169 us
  waiting for transfers between devices  80 us (47%)
  blocking collectives  36.8 us (22%)
  starting transfers between devices  18.5 us (11%)
  Pallas kernels  16.9 us (10%)
  local copies, waits for them, and re-layouts  9.48 us (6%)
  other arithmetic  3.51 us (2%)
  between operations  3.4 us (2%)
    all_to_all x1, waiting for transfers between devices, shards(): lax.all_to_all(shares, 'seq', 0, 0, axis_index_groups=clusters, tiled=True)  53.4 us
    all_to_all x1, blocking collectives, shards(): lax.all_to_all(shares, 'seq', 0, 0, axis_index_groups=clusters, tiled=True)  36.8 us
    ppermute x3, waiting for transfers between devices, crossed(): lax.ppermute(rows, 'seq', [(device_at(cluster, position), device_at((clus...  25.5 us
    pallas_call x1, Pallas kernels, attend(): pl.pallas_call(functools.partial(attention_kernel, cache_tiles, span_tile...  10.4 us
    ppermute x3, starting transfers between devices, crossed(): lax.ppermute(rows, 'seq', [(device_at(cluster, position), device_at((clus...  9.3 us
    all_to_all x1, starting transfers between devices, shards(): lax.all_to_all(shares, 'seq', 0, 0, axis_index_groups=clusters, tiled=True)  9.17 us
    pallas_call x1, Pallas kernels, outgoing(): pl.pallas_call(outgoing_kernel, in_specs=[pl.BlockSpec(memory_space=pltpu...  3.72 us
  transfers between devices with their start and end apart: 5, of which 4 were waited for; matrix products, arithmetic and copies ran while one was open for 1% of the time, Pallas kernels for 0%

profile of v2, /device:TPU:2, one launch (start us, length us, event | category | flops | bytes accessed | tf_op | source)
XLA Modules:
  0.0 168.7 jit_solution(6996419576165578949)
XLA Ops:
  1.3 0.8 copy.18
  2.0 0.6 copy.12
  2.7 0.8 compare_convert_fusion
  3.4 1.3 pad.4.new_ref
  4.8 0.6 pad_add_fusion.live_ref
  5.3 10.4 %shard_map.95 = bf16[32,32,2176]{2,1,0:T(8,128)(2,1)} custom-call(s32[4]{0:T(128)} %pad_add_fusion.live_ref, bf16[128,128]{1,0:T(8,128)(2,1)} %bitcast.33, bf16[1024,2048]{1,0:T(8,128)(2,1)} %cache_ref.1, bf16[1024,2048]{1,0:T(8,128)(2,1)} %bitcast.31, bf16[16,2048]{1,0:T(8,128)(2,1)} %pad.4.new_ref), custom_call_target="tpu_custom_call" | custom-call | flops 2147483648 | bytes 8388608 | tf_op jit(solution)/shard_map/pallas_call | solution.py:161
  15.8 0.0 copy-start.16
  15.8 0.0 copy-start.15
  15.8 0.0 copy-start.17
  15.8 9.2 %all-to-all-start = ((bf16[32,32,2176]{2,1,0:T(8,128)(2,1)}), bf16[32,32,2176]{2,1,0:T(8,128)(2,1)}, u32[]{:S(2)}, u32[]{:S(2)}) async-start(bf16[32,32,2176]{2,1,0:T(8,128)(2,1)} %shard_map.95), calls=%async_computation | async-start | bytes 8912896 | tf_op jit(solution)/shard_map/all_to_all | solution.py:330
  25.0 0.0 copy-done.16
  25.0 0.0 copy-done.15
  25.0 0.6 iota_reduce_fusion
  25.7 0.2 convert_reduce_fusion
  25.9 0.6 fusion.3
  26.5 0.0 collective-permute-start.15
  26.6 1.2 collective-permute-done.15
  29.1 0.0 copy-done.17
  29.1 0.6 fusion.4
  30.4 53.4 %all-to-all-done = bf16[32,32,2176]{2,1,0:T(8,128)(2,1)} async-done(((bf16[32,32,2176]{2,1,0:T(8,128)(2,1)}), bf16[32,32,2176]{2,1,0:T(8,128)(2,1)}, u32[]{:S(2)}, u32[]{:S(2)}) %all-to-all-start) | async-done | bytes 4456480 | tf_op jit(solution)/shard_map/all_to_all | solution.py:330
  83.8 42.9 %conditional.1 = (bf16[32,16,2176]{2,1,0:T(8,128)(2,1)S(1)}) conditional(s32[]{:T(128)} %clamp.3, (s32[8,32]{1,0:T(8,128)S(1)}, bf16[32,32,2176]{2,1,0:T(8,128)(2,1)}) %tuple.25, (s32[8,32]{1,0:T(8,128)S(1)}, bf16[32,32,2176]{2,1,0:T(8,128)(2,1)}) %tuple.25, (s32[8,32]{1,0:T(8,128)S(1)}, ...), branch_computations={%region_4.5_spmd, %region_5.6_spmd, %region_6.7_spmd, %region_7.8_... | conditional | flops 2097152 | bytes 50856120 | solution.py:356
  83.8 3.7 %branch_1_fun.2 = (bf16[80,2176]{1,0:T(8,128)(2,1)}, bf16[80,2176]{1,0:T(8,128)(2,1)}, bf16[80,2176]{1,0:T(8,128)(2,1)}) custom-call(s32[8,32]{1,0:T(8,128)S(1)} %get-tuple-element.31.route_ref, bf16[32,32,2176]{2,1,0:T(8,128)(2,1)} %get-tuple-element.32.arrived_ref), custom_call_target="tpu_custom_call" | custom-call | flops 1048576 | bytes 2097152 | tf_op jit(solution)/shard_map/cond/branch_1_fun/pallas_call | solution.py:217
  87.5 6.4 %collective-permute-start.4 = (bf16[80,2176]{1,0:T(8,128)(2,1)}, bf16[80,2176]{1,0:T(8,128)(2,1)S(1)}, u32[]{:S(2)}, u32[]{:S(2)}) collective-permute-start(bf16[80,2176]{1,0:T(8,128)(2,1)} %get-tuple-element.34), channel_id=1, source_target_pairs={{0,16},{1,17},{2,18},{3,19},{4,20},{5,21},{6,22},{7,23},{32,48},{3... | collective-permute-start | bytes 1044488 | tf_op jit(solution)/shard_map/cond/branch_1_fun/ppermute | solution.py:297
  93.9 0.6 collective-permute-start.5
  94.4 2.4 %collective-permute-start.3 = (bf16[80,2176]{1,0:T(8,128)(2,1)}, bf16[80,2176]{1,0:T(8,128)(2,1)S(1)}, u32[]{:S(2)}, u32[]{:S(2)}) collective-permute-start(bf16[80,2176]{1,0:T(8,128)(2,1)} %get-tuple-element.33.sent_ref), channel_id=1, source_target_pairs={{0,8},{1,9},{2,10},{3,11},{4,12},{5,13},{6,14},{7,15},{32,40},{33,... | collective-permute-start | bytes 1044488 | tf_op jit(solution)/shard_map/cond/branch_1_fun/ppermute | solution.py:297
  96.8 13.4 %collective-permute-done.4.refs_1_ = bf16[80,2176]{1,0:T(8,128)(2,1)S(1)} collective-permute-done((bf16[80,2176]{1,0:T(8,128)(2,1)}, bf16[80,2176]{1,0:T(8,128)(2,1)S(1)}, u32[]{:S(2)}, u32[]{:S(2)}) %collective-permute-start.4) | collective-permute-done | bytes 348192 | tf_op jit(solution)/shard_map/cond/branch_1_fun/ppermute | solution.py:297
  110.2 0.0 copy-start.9
  110.2 12.1 %collective-permute-done.5.refs_2_ = bf16[80,2176]{1,0:T(8,128)(2,1)S(1)} collective-permute-done((bf16[80,2176]{1,0:T(8,128)(2,1)}, bf16[80,2176]{1,0:T(8,128)(2,1)S(1)}, u32[]{:S(2)}, u32[]{:S(2)}) %collective-permute-start.5) | collective-permute-done | bytes 348192 | tf_op jit(solution)/shard_map/cond/branch_1_fun/ppermute | solution.py:297
  122.3 0.0 copy-start.10
  122.3 0.0 collective-permute-done.3.refs_0_
  122.3 0.0 copy-done.9
  122.3 0.7 copy-done.10
  123.0 0.0 copy-start.11
  123.0 0.7 copy-done.11
  123.8 2.7 %branch_1_fun.3 = bf16[32,16,2176]{2,1,0:T(8,128)(2,1)S(1)} custom-call(s32[8,32]{1,0:T(8,128)S(1)} %get-tuple-element.31.route_ref, bf16[32,32,2176]{2,1,0:T(8,128)(2,1)} %get-tuple-element.32.arrived_ref, bf16[80,2176]{1,0:T(8,128)(2,1)} %get-tuple-element.33.sent_ref, bf16[80,2176]{1,0:T(8,128)(2,1)} %copy-done.11, bf16[80,2176]{1,0:T(8,128)(2,1)} %copy-done.9, ...), custom_call_target="tpu_custom_call" | custom-call | flops 1048576 | bytes 4194304 | tf_op jit(solution)/shard_map/cond/branch_1_fun/pallas_call | solution.py:280
  126.7 36.8 %all_to_all.10 = bf16[32,16,2176]{2,1,0:T(8,128)(2,1)S(1)} all-to-all(bf16[32,16,2176]{2,1,0:T(8,128)(2,1)S(1)} %get-tuple-element.63), channel_id=1, replica_groups={{0,1,2,3,4,5,6,7,32,33,34,35,36,37,38,39,64,65,66,67,68,69,70,71,96,97,..., dimensions={0} | all-to-all | bytes 4456448 | tf_op jit(solution)/shard_map/all_to_all | solution.py:359
  163.5 0.0 copy-start
  163.5 1.4 copy-done
  164.9 0.6 copy.15
  165.6 3.2 %slice.9 = bf16[32,16,2048]{2,1,0:T(8,128)(2,1)} slice(bf16[32,16,2176]{2,1,0:T(8,128)(2,1)} %copy-done), slice={[0:32], [0:16], [0:2048]} | slice | bytes 4194304 | tf_op jit(solution)/shard_map/slice | solution.py:361
  (10 shorter events, 0.1 us)
Async XLA Ops:
  15.8 9.2 %copy-start.16 = (s32[32]{0:T(128)S(1)}, s32[32]{0:T(128)}, u32[]{:S(2)}) copy-start(s32[32]{0:T(128)} %param.19) | copy-start | bytes 388
  15.8 9.2 %copy-start.15 = (s32[256]{0:T(256)S(1)}, s32[256]{0:T(256)}, u32[]{:S(2)}) copy-start(s32[256]{0:T(256)} %param.18) | copy-start | bytes 3076
  15.8 13.3 %copy-start.17 = (s32[4]{0:T(128)S(1)}, s32[4]{0:T(128)}, u32[]{:S(2)}) copy-start(s32[4]{0:T(128)} %constant.141.clone) | copy-start | bytes 52
  15.8 68.0 %all-to-all-start = ((bf16[32,32,2176]{2,1,0:T(8,128)(2,1)}), bf16[32,32,2176]{2,1,0:T(8,128)(2,1)}, u32[]{:S(2)}, u32[]{:S(2)}) async-start(bf16[32,32,2176]{2,1,0:T(8,128)(2,1)} %shard_map.95), calls=%async_computation | async-start | bytes 8912896 | tf_op jit(solution)/shard_map/all_to_all | solution.py:330
  26.5 1.2 collective-permute-start.15
  87.5 22.7 %collective-permute-start.4 = (bf16[80,2176]{1,0:T(8,128)(2,1)}, bf16[80,2176]{1,0:T(8,128)(2,1)S(1)}, u32[]{:S(2)}, u32[]{:S(2)}) collective-permute-start(bf16[80,2176]{1,0:T(8,128)(2,1)} %get-tuple-element.34), channel_id=1, source_target_pairs={{0,16},{1,17},{2,18},{3,19},{4,20},{5,21},{6,22},{7,23},{32,48},{3... | collective-permute-start | bytes 1044488 | tf_op jit(solution)/shard_map/cond/branch_1_fun/ppermute | solution.py:297
  93.9 28.4 %collective-permute-start.5 = (bf16[80,2176]{1,0:T(8,128)(2,1)}, bf16[80,2176]{1,0:T(8,128)(2,1)S(1)}, u32[]{:S(2)}, u32[]{:S(2)}) collective-permute-start(bf16[80,2176]{1,0:T(8,128)(2,1)} %get-tuple-element.35), channel_id=1, source_target_pairs={{0,24},{1,25},{2,26},{3,27},{4,28},{5,29},{6,30},{7,31},{32,56},{3... | collective-permute-start | bytes 1044488 | tf_op jit(solution)/shard_map/cond/branch_1_fun/ppermute | solution.py:297
  94.4 27.8 %collective-permute-start.3 = (bf16[80,2176]{1,0:T(8,128)(2,1)}, bf16[80,2176]{1,0:T(8,128)(2,1)S(1)}, u32[]{:S(2)}, u32[]{:S(2)}) collective-permute-start(bf16[80,2176]{1,0:T(8,128)(2,1)} %get-tuple-element.33.sent_ref), channel_id=1, source_target_pairs={{0,8},{1,9},{2,10},{3,11},{4,12},{5,13},{6,14},{7,15},{32,40},{33,... | collective-permute-start | bytes 1044488 | tf_op jit(solution)/shard_map/cond/branch_1_fun/ppermute | solution.py:297
  110.2 12.1 %copy-start.9 = (bf16[80,2176]{1,0:T(8,128)(2,1)}, bf16[80,2176]{1,0:T(8,128)(2,1)S(1)}, u32[]{:S(2)}) copy-start(bf16[80,2176]{1,0:T(8,128)(2,1)S(1)} %collective-permute-done.4.refs_1_) | copy-start | bytes 1044484 | tf_op jit(solution)/shard_map/cond
  122.3 0.7 copy-start.10
  123.0 0.7 copy-start.11
  163.5 1.4 copy-start
